TPU v7x, 32 devices: a whole 2x2x4 slice. The times are simulated.
32 devices in a mesh: groups: 2 (over y), seq: 4 (over z), head: 2 (over x), sub: 2 (over core).
Axes of the slice: x: 2, y: 2, z: 4, core: 2. Of those that a mesh axis runs over, the one named last changes fastest.
Arguments:
- queries: bfloat16 [6144, 3072], P(('groups', 'seq', 'sub'), 'head'), parts along dimension 0, may hold values from -6 to 6
- keys: bfloat16 [6144, 3072], P(('groups', 'seq', 'sub'), 'head'), parts along dimension 0, may hold values from -6 to 6
- values: bfloat16 [6144, 3072], P(('groups', 'seq', 'sub'), 'head'), parts along dimension 0, may hold values from -6 to 6
- kv_list: int32 [16, 6], P(('groups', 'seq', 'sub')), parts along dimension 0, may hold values from -1 to 7, as said below
- kv_count: int32 [16], P(('groups', 'seq', 'sub')), parts along dimension 0, may hold values from 1 to 6, as said below
- out_weight: bfloat16 [3072, 3072], P('head'), may hold values from -0.5 to 0.5
- gate: float32 [3072], P('head'), may hold values from 1 to 4
Outputs:
- layer_out: bfloat16 [6144, 3072], P(('groups', 'seq', 'sub'), 'head'), parts along dimension 0
There are 2 independent parts, one for each index of `groups`. A program takes and returns all parts, laid end to end along the dimension named above; an argument that names none is the same for every part. Nothing has to cross between parts.
Inputs may be any that keep to these rules, and one draw needn't show every extreme that they name: `kv_list`: tile t lies at time t // 2 and height t % 2 of a slab of 4 x 2 x 1 tiles. Row t begins with t itself, then lists in a drawn order the other tiles of t's 3 x 3 x 3 window clipped to the slab (time within one of t's), then -1 in the entries left over. `kv_count`: at most the number of tiles in the row's clipped window; some tile has 6 and some tile has 1.
All inputs are finite; a program needn't handle non-finite values.
Results may differ from a plain program's by a relative error of at most 0.014.
Values may be sent and summed in bfloat16 or wider, within the bound.
A program may use at most 128 MiB of HBM per device.

v0:
```python
import math

import jax
import jax.numpy as jnp
from jax import lax
from jax.sharding import PartitionSpec as P

HD = 128
REACH = 3


NEG_FILL = -1e30


def shifted(block, axis, distance):
    devices = range(lax.axis_size(axis))
    route = [(i - distance, i) for i in devices if i - distance in devices]
    return lax.ppermute(block, axis, route)


def tile_scores(query_tiles, key_tiles):
    scores = jnp.einsum(
        "aqhd,bkhd->abhqk", query_tiles, key_tiles, preferred_element_type=jnp.float32
    )
    return scores * (1.0 / math.sqrt(query_tiles.shape[-1]))


def local(queries, keys, values, kv_list, kv_count, out_weight, gate):
    tiles_here = kv_list.shape[0]
    tile_rows = queries.shape[0] // tiles_here
    width = queries.shape[1]
    heads_here = width // HD
    query_tiles = queries.reshape(tiles_here, tile_rows, heads_here, HD)
    kv_pair = jnp.stack([keys, values])
    position = lax.axis_index(("seq", "sub"))
    places = lax.axis_size(("seq", "sub"))
    blocks = [(position, kv_pair)]
    for offset in range(1, REACH + 1):
        for heading in (offset, -offset):
            blocks.append((position - heading, shifted(kv_pair, ("seq", "sub"), heading)))
    live_slots = jnp.arange(kv_list.shape[1])[None, :] < kv_count[:, None]

    def included(anchor):
        inside = (anchor >= 0) & (anchor < places)
        neighbour = anchor * tiles_here + jnp.arange(tiles_here, dtype=jnp.int32)
        hits = (kv_list[:, :, None] == neighbour[None, None, :]) & live_slots[:, :, None]
        return jnp.any(hits, axis=1) & inside

    peak = jnp.full((tiles_here, heads_here, tile_rows), NEG_FILL, jnp.float32)
    for anchor, fetched in blocks:
        block_mask = included(anchor)
        block_key_tiles = fetched[0].reshape(tiles_here, tile_rows, heads_here, HD)
        scores = jnp.where(
            block_mask[:, :, None, None, None], tile_scores(query_tiles, block_key_tiles), NEG_FILL
        )
        peak = jnp.maximum(peak, jnp.max(scores, axis=(1, 4)))
    state = (
        jnp.zeros((tiles_here, tile_rows, heads_here, HD), jnp.float32),
        jnp.zeros((tiles_here, heads_here, tile_rows), jnp.float32),
    )
    for anchor, fetched in blocks:
        mask = included(anchor)
        key_tiles = fetched[0].reshape(tiles_here, tile_rows, heads_here, HD)
        value_tiles = fetched[1].reshape(tiles_here, tile_rows, heads_here, HD)
        compute_accum, compute_total = state
        compute_scores = jnp.where(
            mask[:, :, None, None, None], tile_scores(query_tiles, key_tiles), NEG_FILL
        )
        weights = jnp.exp(compute_scores - peak[:, None, :, :, None])
        compute_total = compute_total + jnp.sum(weights, axis=(1, 4))
        compute_accum = compute_accum + jnp.einsum(
            "abhqk,bkhd->aqhd",
            weights.astype(jnp.bfloat16),
            value_tiles,
            preferred_element_type=jnp.float32,
        )
        state = (compute_accum, compute_total)
    accum, total = state
    attention = (
        (accum / jnp.transpose(total, (0, 2, 1))[:, :, :, None])
        .reshape(tiles_here * tile_rows, width)
        .astype(jnp.bfloat16)
    )
    summed = lax.psum_scatter(
        lax.dot_general(
            out_weight, attention, (((0,), (1,)), ((), ())), preferred_element_type=jnp.float32
        ).astype(jnp.bfloat16),
        "head",
        scatter_dimension=0,
        tiled=True,
    ).astype(jnp.float32)
    return (jnp.transpose(summed) * gate[None, :]).astype(jnp.bfloat16)


def solution(mesh):
    return jax.shard_map(
        local,
        mesh=mesh,
        in_specs=(
            P(("groups", "seq", "sub"), "head"),
            P(("groups", "seq", "sub"), "head"),
            P(("groups", "seq", "sub"), "head"),
            P(("groups", "seq", "sub"), None),
            P(("groups", "seq", "sub")),
            P("head", None),
            P("head"),
        ),
        out_specs=P(("groups", "seq", "sub"), "head"),
        check_vma=False,
    )
```

profile of v0, /device:TPU:0, one launch (start us, length us, event | category | flops | bytes accessed | tf_op | source)
XLA Modules:
  0.0 282.6 jit_solution(356027137580236161)
XLA Ops:
  6.5 1.8 copy.30
  8.3 0.0 copy-done.5
  8.4 0.7 copy.35
  9.1 1.7 pad_maximum_fusion
  10.8 1.4 collective-permute-start.5
  12.2 1.3 collective-permute-start.3
  13.5 7.0 %collective-permute-start.2 = (bf16[2,384,1536]{1,2,0:T(8,128)(2,1)}, bf16[2,384,1536]{1,2,0:T(8,128)(2,1)}, u32[]{:S(2)}, u32[]{:S(2)}) collective-permute-start(bf16[2,384,1536]{1,2,0:T(8,128)(2,1)} %pad_maximum_fusion), channel_id=1, source_target_pairs={{0,4},{1,5},{4,8},{5,9},{8,12},{9,13},{2,6},{3,7},{6,10},{7,11},{1... | collective-permute-start | bytes 7077896 | tf_op jit(solution)/shard_map/ppermute | solution.py:18
  20.5 1.3 collective-permute-start.1
  21.8 4.5 %collective-permute-start = (bf16[2,384,1536]{1,2,0:T(8,128)(2,1)}, bf16[2,384,1536]{1,2,0:T(8,128)(2,1)}, u32[]{:S(2)}, u32[]{:S(2)}) collective-permute-start(bf16[2,384,1536]{1,2,0:T(8,128)(2,1)} %pad_maximum_fusion), channel_id=1, source_target_pairs={{0,1},{1,4},{4,5},{5,8},{8,9},{9,12},{12,13},{2,3},{3,6},{6,7},{7,... | collective-permute-start | bytes 7077896 | tf_op jit(solution)/shard_map/ppermute | solution.py:18
  27.0 1.7 copy.31
  28.7 0.8 and_reduce_fusion.6
  33.9 1.2 bitcast_reduce_fusion.6
  35.1 51.6 %collective-permute-done.5 = bf16[2,384,1536]{1,2,0:T(8,128)(2,1)} collective-permute-done((bf16[2,384,1536]{1,2,0:T(8,128)(2,1)}, bf16[2,384,1536]{1,2,0:T(8,128)(2,1)}, u32[]{:S(2)}, u32[]{:S(2)}) %collective-permute-start.5) | collective-permute-done | bytes 2359328 | tf_op jit(solution)/shard_map/ppermute | solution.py:18
  86.7 1.6 collective-permute-start.4
  88.3 1.9 fusion.94
  90.2 1.2 bitcast_reduce_fusion
  91.4 3.4 %collective-permute-done.3 = bf16[2,384,1536]{1,2,0:T(8,128)(2,1)} collective-permute-done((bf16[2,384,1536]{1,2,0:T(8,128)(2,1)}, bf16[2,384,1536]{1,2,0:T(8,128)(2,1)}, u32[]{:S(2)}, u32[]{:S(2)}) %collective-permute-start.3) | collective-permute-done | bytes 2359328 | tf_op jit(solution)/shard_map/ppermute | solution.py:18
  94.8 1.9 fusion.98
  96.6 1.2 bitcast_reduce_fusion.2
  97.9 0.0 collective-permute-done.2
  97.9 3.6 %fusion.97 = (bf16[1,384,1536]{1,2,0:T(8,128)(2,1)S(1)}, bf16[1,384,1536]{1,2,0:T(8,128)(2,1)S(1)}) fusion(bf16[2,384,1536]{1,2,0:T(8,128)(2,1)} %collective-permute-done.2), kind=kLoop, calls=%fused_computation.124 | loop fusion | bytes 4718592 | tf_op jit(solution)/shard_map/slice | solution.py:64
  101.5 1.2 bitcast_reduce_fusion.3
  102.7 0.0 collective-permute-done.1
  102.7 3.6 %fusion.96 = (bf16[1,384,1536]{1,2,0:T(8,128)(2,1)S(1)}, bf16[1,384,1536]{1,2,0:T(8,128)(2,1)S(1)}) fusion(bf16[2,384,1536]{1,2,0:T(8,128)(2,1)} %collective-permute-done.1), kind=kLoop, calls=%fused_computation.123 | loop fusion | bytes 4718592 | tf_op jit(solution)/shard_map/slice | solution.py:64
  106.4 4.0 %bitcast_reduce_fusion.4 = (f32[12,384]{1,0:T(8,128)S(1)}, f32[12,384,384]{2,1,0:T(8,128)}) fusion(pred[]{:T(512)S(6)} %and.136, bf16[384,12,128]{0,2,1:T(8,128)(2,1)S(1)} %bitcast.212, bf16[384,12,128]{0,2,1:T(8,128)(2,1)S(1)} %bitcast.200), kind=kOutput, calls=%fused_computation.13 | convolution fusion | flops 458288640 | bytes 9455617 | tf_op jit(solution)/shard_map/aqhd,bkhd->abhqk/dot_general | solution.py:22
  110.4 0.0 collective-permute-done
  110.4 2.9 %fusion.95 = (bf16[1,384,1536]{1,2,0:T(8,128)(2,1)}, bf16[1,384,1536]{1,2,0:T(8,128)(2,1)S(1)}) fusion(bf16[2,384,1536]{1,2,0:T(8,128)(2,1)} %collective-permute-done), kind=kLoop, calls=%fused_computation.122 | loop fusion | bytes 4718592 | tf_op jit(solution)/shard_map/slice | solution.py:64
  113.3 4.0 %bitcast_reduce_fusion.5 = (f32[12,384]{1,0:T(8,128)S(1)}, f32[12,384,384]{2,1,0:T(8,128)}) fusion(pred[]{:T(512)S(6)} %and.133, bf16[384,12,128]{0,2,1:T(8,128)(2,1)S(1)} %bitcast.213, bf16[384,12,128]{0,2,1:T(8,128)(2,1)S(1)} %bitcast.201), kind=kOutput, calls=%fused_computation.16 | convolution fusion | flops 458288640 | bytes 9455617 | tf_op jit(solution)/shard_map/aqhd,bkhd->abhqk/dot_general | solution.py:22
  117.3 22.7 %collective-permute-done.4 = bf16[2,384,1536]{1,2,0:T(8,128)(2,1)S(1)} collective-permute-done((bf16[2,384,1536]{1,2,0:T(8,128)(2,1)}, bf16[2,384,1536]{1,2,0:T(8,128)(2,1)S(1)}, u32[]{:S(2)}, u32[]{:S(2)}) %collective-permute-start.4) | collective-permute-done | bytes 2359328 | tf_op jit(solution)/shard_map/ppermute | solution.py:18
  140.0 1.2 fusion.99
  141.2 4.1 %bitcast_reduce_fusion.1 = (f32[12,384]{1,0:T(8,128)S(1)}, f32[12,384,384]{2,1,0:T(8,128)}) fusion(pred[]{:T(512)S(6)} %and.145, bf16[384,12,128]{0,2,1:T(8,128)(2,1)S(1)} %bitcast.208, bf16[384,12,128]{0,2,1:T(8,128)(2,1)S(1)} %bitcast.202), kind=kOutput, calls=%fused_computation.4 | convolution fusion | flops 458288640 | bytes 9455617 | tf_op jit(solution)/shard_map/aqhd,bkhd->abhqk/dot_general | solution.py:22
  145.4 0.0 copy-start.7
  145.4 0.0 copy-start.6
  145.4 1.7 fusion.41
  147.1 4.7 %fusion.38 = f32[12,128,384]{2,1,0:T(8,128)S(1)} fusion(bf16[384,12,128]{0,2,1:T(8,128)(2,1)S(1)} %bitcast.219, f32[12,384,384]{2,1,0:T(8,128)} %get-tuple-element.42, f32[12,384]{1,0:T(8,128)S(1)} %maximum_maximum_fusion, pred[]{:T(512)S(6)} %and.133), kind=kOutput, calls=%fused_computation.55 | convolution fusion | flops 460062720 | bytes 10635265 | tf_op jit(solution)/shard_map/abhqk,bkhd->aqhd/dot_general | solution.py:71
  151.9 6.4 %fusion.35 = f32[12,128,384]{2,1,0:T(8,128)} fusion(bf16[384,12,128]{0,2,1:T(8,128)(2,1)S(1)} %bitcast.218, f32[12,384,384]{2,1,0:T(8,128)} %get-tuple-element.40, f32[12,384]{1,0:T(8,128)S(1)} %maximum_maximum_fusion, pred[]{:T(512)S(6)} %and.136), kind=kOutput, calls=%fused_computation.53 | convolution fusion | flops 460062720 | bytes 10635265 | tf_op jit(solution)/shard_map/abhqk,bkhd->aqhd/dot_general | solution.py:71
  158.3 3.1 %fusion.32 = f32[12,128,384]{2,1,0:T(8,128)} fusion(bf16[384,12,128]{0,2,1:T(8,128)(2,1)S(1)} %bitcast.216, f32[12,384,384]{2,1,0:T(8,128)S(1)} %get-tuple-element.38, f32[12,384]{1,0:T(8,128)S(1)} %maximum_maximum_fusion, pred[]{:T(512)S(6)} %and.139), kind=kOutput, calls=%fused_computation.51 | convolution fusion | flops 460062720 | bytes 10635265 | tf_op jit(solution)/shard_map/abhqk,bkhd->aqhd/dot_general | solution.py:71
  161.4 0.0 copy-done.7
  161.4 3.1 %fusion.29 = f32[12,128,384]{2,1,0:T(8,128)} fusion(bf16[384,12,128]{0,2,1:T(8,128)(2,1)S(1)} %bitcast.215, f32[12,384,384]{2,1,0:T(8,128)S(1)} %get-tuple-element.36, f32[12,384]{1,0:T(8,128)S(1)} %maximum_maximum_fusion, pred[]{:T(512)S(6)} %and.142), kind=kOutput, calls=%fused_computation.49 | convolution fusion | flops 460062720 | bytes 10635265 | tf_op jit(solution)/shard_map/abhqk,bkhd->aqhd/dot_general | solution.py:71
  164.5 16.3 %fusion.9 = (f32[12,384]{1,0:T(8,128)S(1)}, f32[12,384]{1,0:T(8,128)S(1)}, f32[12,384]{1,0:T(8,128)S(1)}, f32[12,384]{1,0:T(8,128)S(1)}, f32[12,384]{1,0:T(8,128...) fusion(f32[12,384,384]{2,1,0:T(8,128)} %get-tuple-element.42, f32[12,384]{1,0:T(8,128)} %copy-done.7, pred[]{:T(512)S(6)} %and.133, ...), kind=kLoop, calls=%fused_computation.30 | loop fusion | flops 49512960 | bytes 49692680 | tf_op jit(solution)/shard_map/reduce_sum | solution.py:70
  180.8 0.0 copy-done.8
  180.8 5.2 %fusion.26 = f32[12,128,384]{2,1,0:T(8,128)S(1)} fusion(bf16[384,12,128]{0,2,1:T(8,128)(2,1)} %bitcast.217, f32[12,384,384]{2,1,0:T(8,128)} %get-tuple-element.34, f32[12,384]{1,0:T(8,128)S(1)} %copy-done.8, pred[]{:T(512)S(6)} %and.145), kind=kOutput, calls=%fused_computation.47 | convolution fusion | flops 460062720 | bytes 10635265 | tf_op jit(solution)/shard_map/abhqk,bkhd->aqhd/dot_general | solution.py:71
  186.1 0.2 copy-done.4
  186.2 2.5 fusion.71
  188.7 8.9 %fusion.21 = bf16[3072,384]{0,1:T(8,128)(2,1)} fusion(bf16[384,1536]{0,1:T(8,128)(2,1)S(1)} %bitcast.214, bf16[1536,3072]{1,0:T(8,128)(2,1)} %param.12), kind=kOutput, calls=%fused_computation.43 | convolution fusion | flops 3625058304 | bytes 12976128 | tf_op jit(solution)/shard_map/dot_general | solution.py:85
  197.7 0.0 reduce-scatter.2.cloned.1.call-update
  197.7 75.6 %reduce-scatter.2.cloned.1.call-done = bf16[1536,384]{0,1:T(8,128)(2,1)} async-done(((bf16[3072,384]{0,1:T(8,128)(2,1)}), bf16[1536,384]{0,1:T(8,128)(2,1)}) %reduce-scatter.2.cloned.1.call-update) | async-done | bytes 1179664 | tf_op jit(solution)/shard_map/reduce_scatter | solution.py:84
  273.3 2.5 fusion.77
  (19 shorter events, 0.1 us)
Async XLA Ops:
  6.5 1.8 copy-start.5
  6.5 266.8 %reduce-scatter.2.cloned.1.call-start = ((), (), s32[]{:S(2)}) async-start(), calls=%async_computation.1 | async-start | bytes 3538944 | tf_op jit(solution)/shard_map/reduce_scatter | solution.py:84
  10.8 17.9 %copy-start.10 = (s32[1,6]{1,0:T(1,128)S(1)}, s32[1,6]{1,0:T(1,128)}, u32[]{:S(2)}) copy-start(s32[1,6]{1,0:T(1,128)} %param.10) | copy-start | bytes 76
  10.8 75.9 %collective-permute-start.5 = (bf16[2,384,1536]{1,2,0:T(8,128)(2,1)}, bf16[2,384,1536]{1,2,0:T(8,128)(2,1)}, u32[]{:S(2)}, u32[]{:S(2)}) collective-permute-start(bf16[2,384,1536]{1,2,0:T(8,128)(2,1)} %pad_maximum_fusion), channel_id=1, source_target_pairs={{5,0},{8,1},{9,4},{12,5},{13,8},{7,2},{10,3},{11,6},{14,7},{15,10}... | collective-permute-start | bytes 7077896 | tf_op jit(solution)/shard_map/ppermute | solution.py:18
  12.2 82.5 %collective-permute-start.3 = (bf16[2,384,1536]{1,2,0:T(8,128)(2,1)}, bf16[2,384,1536]{1,2,0:T(8,128)(2,1)}, u32[]{:S(2)}, u32[]{:S(2)}) collective-permute-start(bf16[2,384,1536]{1,2,0:T(8,128)(2,1)} %pad_maximum_fusion), channel_id=1, source_target_pairs={{4,0},{5,1},{8,4},{9,5},{12,8},{13,9},{6,2},{7,3},{10,6},{11,7},{1... | collective-permute-start | bytes 7077896 | tf_op jit(solution)/shard_map/ppermute | solution.py:18
  13.5 84.3 %collective-permute-start.2 = (bf16[2,384,1536]{1,2,0:T(8,128)(2,1)}, bf16[2,384,1536]{1,2,0:T(8,128)(2,1)}, u32[]{:S(2)}, u32[]{:S(2)}) collective-permute-start(bf16[2,384,1536]{1,2,0:T(8,128)(2,1)} %pad_maximum_fusion), channel_id=1, source_target_pairs={{0,4},{1,5},{4,8},{5,9},{8,12},{9,13},{2,6},{3,7},{6,10},{7,11},{1... | collective-permute-start | bytes 7077896 | tf_op jit(solution)/shard_map/ppermute | solution.py:18
  20.5 82.2 %collective-permute-start.1 = (bf16[2,384,1536]{1,2,0:T(8,128)(2,1)}, bf16[2,384,1536]{1,2,0:T(8,128)(2,1)}, u32[]{:S(2)}, u32[]{:S(2)}) collective-permute-start(bf16[2,384,1536]{1,2,0:T(8,128)(2,1)} %pad_maximum_fusion), channel_id=1, source_target_pairs={{1,0},{4,1},{5,4},{8,5},{9,8},{12,9},{13,12},{3,2},{6,3},{7,6},{10... | collective-permute-start | bytes 7077896 | tf_op jit(solution)/shard_map/ppermute | solution.py:18
  21.8 88.6 %collective-permute-start = (bf16[2,384,1536]{1,2,0:T(8,128)(2,1)}, bf16[2,384,1536]{1,2,0:T(8,128)(2,1)}, u32[]{:S(2)}, u32[]{:S(2)}) collective-permute-start(bf16[2,384,1536]{1,2,0:T(8,128)(2,1)} %pad_maximum_fusion), channel_id=1, source_target_pairs={{0,1},{1,4},{4,5},{5,8},{8,9},{9,12},{12,13},{2,3},{3,6},{6,7},{7,... | collective-permute-start | bytes 7077896 | tf_op jit(solution)/shard_map/ppermute | solution.py:18
  86.7 53.3 %collective-permute-start.4 = (bf16[2,384,1536]{1,2,0:T(8,128)(2,1)}, bf16[2,384,1536]{1,2,0:T(8,128)(2,1)S(1)}, u32[]{:S(2)}, u32[]{:S(2)}) collective-permute-start(bf16[2,384,1536]{1,2,0:T(8,128)(2,1)} %pad_maximum_fusion), channel_id=1, source_target_pairs={{0,5},{1,8},{4,9},{5,12},{8,13},{2,7},{3,10},{6,11},{7,14},{10,15}... | collective-permute-start | bytes 7077896 | tf_op jit(solution)/shard_map/ppermute | solution.py:18
  97.9 63.5 %copy-start = (f32[12,384,384]{2,1,0:T(8,128)}, f32[12,384,384]{2,1,0:T(8,128)S(1)}, u32[]{:S(2)}) copy-start(f32[12,384,384]{2,1,0:T(8,128)S(1)} %get-tuple-element.36) | copy-start | bytes 21233668
  102.7 55.5 %copy-start.1 = (f32[12,384,384]{2,1,0:T(8,128)}, f32[12,384,384]{2,1,0:T(8,128)S(1)}, u32[]{:S(2)}) copy-start(f32[12,384,384]{2,1,0:T(8,128)S(1)} %get-tuple-element.38) | copy-start | bytes 21233668
  145.4 16.0 %copy-start.7 = (f32[12,384]{1,0:T(8,128)}, f32[12,384]{1,0:T(8,128)S(1)}, u32[]{:S(2)}) copy-start(f32[12,384]{1,0:T(8,128)S(1)} %maximum_maximum_fusion) | copy-start | bytes 55300
  145.4 1.7 copy-start.6
  164.5 16.3 %copy-start.8 = (f32[12,384]{1,0:T(8,128)S(1)}, f32[12,384]{1,0:T(8,128)}, u32[]{:S(2)}) copy-start(f32[12,384]{1,0:T(8,128)} %copy-done.7) | copy-start | bytes 55300
  180.8 5.3 %copy-start.2 = (f32[12,128,384]{2,1,0:T(8,128)S(1)}, f32[12,128,384]{2,1,0:T(8,128)}, u32[]{:S(2)}) copy-start(f32[12,128,384]{2,1,0:T(8,128)} %fusion.35) | copy-start | bytes 7077892
  180.8 5.3 %copy-start.3 = (f32[12,128,384]{2,1,0:T(8,128)S(1)}, f32[12,128,384]{2,1,0:T(8,128)}, u32[]{:S(2)}) copy-start(f32[12,128,384]{2,1,0:T(8,128)} %fusion.32) | copy-start | bytes 7077892
  180.8 5.4 %copy-start.4 = (f32[12,128,384]{2,1,0:T(8,128)S(1)}, f32[12,128,384]{2,1,0:T(8,128)}, u32[]{:S(2)}) copy-start(f32[12,128,384]{2,1,0:T(8,128)} %fusion.29) | copy-start | bytes 7077892
  197.6 75.7 %copy-start.9 = (f32[1536]{0:T(1024)S(1)}, f32[1536]{0:T(1024)}, u32[]{:S(2)}) copy-start(f32[1536]{0:T(1024)} %param.13) | copy-start | bytes 18436
Sparse Core Ops, SparseCore 0:
  197.8 75.4 reduce-scatter.1
where the time goes:
time: 283 us
  waiting for transfers between devices  153 us (54%)
  matrix products  52.7 us (19%)
  other arithmetic  21.3 us (8%)
  local copies, waits for them, and re-layouts  19.6 us (7%)
  between operations  18.6 us (7%)
  starting transfers between devices  17.1 us (6%)
    ppermute x6, waiting for transfers between devices, shifted(): return lax.ppermute(block, axis, route)  77.7 us
    reduce_scatter x1, waiting for transfers between devices, local(): lax.psum_scatter(lax.dot_general(out_weight, attention, (((0,), (1,)), ((...  75.6 us
    dot_general x7, matrix products, local(): jnp.einsum('abhqk,bkhd->aqhd', weights.astype(jnp.bfloat16), value_tiles,...  26.8 us
    ppermute x6, starting transfers between devices, shifted(): return lax.ppermute(block, axis, route)  17.1 us
    dot_general x7, matrix products, tile_scores(): jnp.einsum('aqhd,bkhd->abhqk', query_tiles, key_tiles, preferred_element_...  17 us
    reduce_sum x1, other arithmetic, local(): compute_total = compute_total + jnp.sum(weights, axis=(1, 4))  16.3 us
    slice x5, local copies, waits for them, and re-layouts, local(): value_tiles = fetched[1].reshape(tiles_here, tile_rows, heads_here, HD)  13.9 us
    dot_general x1, matrix products, local(): lax.dot_general(out_weight, attention, (((0,), (1,)), ((), ())), preferre...  8.94 us
  transfers between devices with their start and end apart: 7, of which 4 were waited for; matrix products, arithmetic and copies ran while one was open for 10% of the time, Pallas kernels for 0%

commit v1 on v0

--- a/solution.py
+++ b/solution.py
@@ -3,6 +3,8 @@
 import jax
 import jax.numpy as jnp
 from jax import lax
+from jax.experimental import pallas as pl
+from jax.experimental.pallas import tpu as pltpu
 from jax.sharding import PartitionSpec as P
 
 HD = 128
@@ -92,9 +94,346 @@
     return (jnp.transpose(summed) * gate[None, :]).astype(jnp.bfloat16)
 
 
+HEADS_PER_CHUNK = 2
+AHEAD = 3
+WEIGHT_PIECES = 3
+MESH = pl.DeviceIdType.MESH
+
+
+def fused_kernel(
+    q_hbm, k_hbm, v_hbm, list_ref, count_ref, w_hbm, gate_ref, out_ref,
+    q_buf, kv, att, w_own, w_rem, acc,
+    kv_in, q_in, w_in, kv_send, kv_recv, att_send, att_recv, w_send, w_recv,
+):
+    chunks = kv.shape[1]
+    cols = kv.shape[4]
+    width = q_buf.shape[1]
+    quarter = w_rem.shape[2]
+    piece_rows = width // WEIGHT_PIECES
+    y, z = lax.axis_index("groups"), lax.axis_index("seq")
+    x, s = lax.axis_index("head"), lax.axis_index("sub")
+    z_size = lax.axis_size("seq")
+    has_low, has_high = z > 0, z < z_size - 1
+    core, across, other = {"sub": 1 - s}, {"head": 1 - x}, {"groups": 1 - y}
+    low, high = {"seq": z - 1}, {"seq": z + 1}
+
+    def lanes(start, size):
+        return pl.ds(pl.multiple_of(start, HD), size)
+
+    def own_in(c, which):
+        src = (k_hbm, v_hbm)[which]
+        return pltpu.make_async_copy(
+            src.at[:, lanes(c * cols, cols)], kv.at[0, c, which], kv_in.at[c, which]
+        )
+
+    def kv_copy(way, src_slot, dst_slot, c, device):
+        return pltpu.make_async_remote_copy(
+            src_ref=kv.at[src_slot, c], dst_ref=kv.at[dst_slot, c],
+            send_sem=kv_send.at[way, c], recv_sem=kv_recv.at[dst_slot, c],
+            device_id=device, device_id_type=MESH,
+        )
+
+    def up(c):
+        return kv_copy(0, 0, 2, c, high)
+
+    def down(c):
+        return kv_copy(1, 0, 4, c, low)
+
+    def side(c):
+        return kv_copy(2, 0, 1, c, core)
+
+    def side_low(c):
+        return kv_copy(3, 2, 3, c, core)
+
+    def side_high(c):
+        return kv_copy(4, 4, 5, c, core)
+
+    def arrived(slot, c):
+        kv_copy(2, 0, slot, c, core).wait_recv()
+
+    def att_copy(c):
+        piece = lanes(c * cols, cols)
+        return pltpu.make_async_remote_copy(
+            src_ref=att.at[0, :, piece], dst_ref=att.at[1, :, piece],
+            send_sem=att_send.at[c], recv_sem=att_recv.at[c],
+            device_id=across, device_id_type=MESH,
+        )
+
+    mine, theirs = y * 2 + s, (1 - y) * 2 + s
+
+    def w_across(p):
+        rows = pl.ds(p * piece_rows, piece_rows)
+        return pltpu.make_async_remote_copy(
+            src_ref=w_hbm.at[rows, lanes((1 - x) * width + mine * quarter, quarter)],
+            dst_ref=w_rem.at[mine, rows], send_sem=w_send.at[0, p], recv_sem=w_recv.at[0, p],
+            device_id=across, device_id_type=MESH,
+        )
+
+    def w_forward(way, place, p, device):
+        rows = pl.ds(p * piece_rows, piece_rows)
+        return pltpu.make_async_remote_copy(
+            src_ref=w_rem.at[place, rows], dst_ref=w_rem.at[place, rows],
+            send_sem=w_send.at[way, p], recv_sem=w_recv.at[way, p],
+            device_id=device, device_id_type=MESH,
+        )
+
+    def w_other(p):
+        return w_forward(1, mine, p, other)
+
+    def w_side(p):
+        return w_forward(2, mine, p, core)
+
+    def w_side_other(p):
+        return w_forward(3, theirs, p, core)
+
+    q_copy = pltpu.make_async_copy(q_hbm, q_buf, q_in)
+    w_copy = pltpu.make_async_copy(w_hbm.at[:, lanes(x * width, width)], w_own, w_in)
+
+    @pl.loop(0, chunks)
+    def _(c):
+        own_in(c, 0).start()
+        own_in(c, 1).start()
+
+    q_copy.start()
+
+    barrier = pltpu.get_barrier_semaphore()
+    for device in (core, across, other):
+        pl.semaphore_signal(barrier, inc=1, device_id=device, device_id_type=MESH)
+
+    @pl.when(has_low)
+    def _():
+        pl.semaphore_signal(barrier, inc=1, device_id=low, device_id_type=MESH)
+
+    @pl.when(has_high)
+    def _():
+        pl.semaphore_signal(barrier, inc=1, device_id=high, device_id_type=MESH)
+
+    pl.semaphore_wait(barrier, 3 + (z > 0).astype(jnp.int32) + (z < z_size - 1).astype(jnp.int32))
+
+    def send_along(c):
+        @pl.when(has_high)
+        def _():
+            up(c).start()
+
+        @pl.when(has_low)
+        def _():
+            down(c).start()
+
+    @pl.loop(0, chunks)
+    def _(c):
+        own_in(c, 0).wait()
+        own_in(c, 1).wait()
+
+        @pl.when(c < AHEAD)
+        def _():
+            send_along(c)
+
+    @pl.loop(0, WEIGHT_PIECES)
+    def _(p):
+        w_across(p).start()
+
+    @pl.loop(0, chunks)
+    def _(c):
+        side(c).start()
+
+    w_copy.start()
+
+    @pl.when(jnp.logical_not(has_low))
+    def _():
+        @pl.loop(0, chunks)
+        def _(c):
+            kv[2, c] = jnp.zeros(kv.shape[2:], kv.dtype)
+            kv[3, c] = jnp.zeros(kv.shape[2:], kv.dtype)
+
+    @pl.when(jnp.logical_not(has_high))
+    def _():
+        @pl.loop(0, chunks)
+        def _(c):
+            kv[4, c] = jnp.zeros(kv.shape[2:], kv.dtype)
+            kv[5, c] = jnp.zeros(kv.shape[2:], kv.dtype)
+
+    tiles = [
+        z * 2 + s, z * 2 + 1 - s,
+        z * 2 - 2 + s, z * 2 - 1 - s,
+        z * 2 + 2 + s, z * 2 + 3 - s,
+    ]
+    count = count_ref[0]
+    biases = []
+    for slot, tile in enumerate(tiles):
+        bias = jnp.float32(NEG_FILL)
+        for j in range(list_ref.shape[1]):
+            hit = (list_ref[0, j] == tile) & (j < count)
+            bias = jnp.where(hit, jnp.float32(0.0), bias)
+        if slot in (2, 3):
+            bias = jnp.where(has_low, bias, jnp.float32(NEG_FILL))
+        if slot in (4, 5):
+            bias = jnp.where(has_high, bias, jnp.float32(NEG_FILL))
+        biases.append(bias)
+    factor = (1.0 / math.sqrt(HD)) * math.log2(math.e)
+    q_copy.wait()
+
+    @pl.loop(0, chunks)
+    def _(c):
+        @pl.when(has_low)
+        def _():
+            arrived(2, c)
+            side_low(c).start()
+
+        @pl.when(has_high)
+        def _():
+            arrived(4, c)
+            side_high(c).start()
+
+        @pl.when(c + AHEAD < chunks)
+        def _():
+            send_along(c + AHEAD)
+
+        @pl.when((c >= 1) & (c < 1 + WEIGHT_PIECES))
+        def _():
+            w_across(c - 1).wait_recv()
+            w_other(c - 1).start()
+            w_side(c - 1).start()
+
+        @pl.when((c >= 3) & (c < 3 + WEIGHT_PIECES))
+        def _():
+            w_other(c - 3).wait_recv()
+            w_side_other(c - 3).start()
+
+        arrived(1, c)
+
+        @pl.when(has_low)
+        def _():
+            arrived(3, c)
+
+        @pl.when(has_high)
+        def _():
+            arrived(5, c)
+
+        for h in range(cols // HD):
+            head = pl.ds(h * HD, HD)
+            place = lanes(c * cols + h * HD, HD)
+            query = q_buf[:, place]
+            scores = [
+                lax.dot_general(
+                    query, kv[t, c, 0, :, head], (((1,), (1,)), ((), ())),
+                    preferred_element_type=jnp.float32,
+                )
+                for t in range(6)
+            ]
+            peak = None
+            for t in range(6):
+                top = jnp.max(scores[t], axis=1, keepdims=True) * factor + biases[t]
+                peak = top if peak is None else jnp.maximum(peak, top)
+            total, mixed = None, None
+            for t in range(6):
+                weights = jnp.exp2(scores[t] * factor - (peak - biases[t]))
+                part = jnp.sum(weights, axis=1, keepdims=True)
+                term = jnp.dot(
+                    weights.astype(jnp.bfloat16), kv[t, c, 1, :, head],
+                    preferred_element_type=jnp.float32,
+                )
+                total = part if total is None else total + part
+                mixed = term if mixed is None else mixed + term
+            att[0, :, place] = (mixed / total).astype(jnp.bfloat16)
+        att_copy(c).start()
+
+    w_copy.wait()
+    for q in range(4):
+        span = pl.ds(q * quarter, quarter)
+        acc[:, span] = jnp.dot(att[0], w_own[:, span], preferred_element_type=jnp.float32)
+
+    @pl.loop(0, WEIGHT_PIECES)
+    def _(p):
+        w_side(p).wait_recv()
+        w_side_other(p).wait_recv()
+
+    @pl.loop(0, chunks - 1)
+    def _(c):
+        att_copy(c).wait_recv()
+
+    early = (chunks - 1) * cols
+    for q in range(4):
+        span = pl.ds(q * quarter, quarter)
+        acc[:, span] += jnp.dot(
+            att[1, :, :early], w_rem[q, :early, :], preferred_element_type=jnp.float32
+        )
+    att_copy(chunks - 1).wait_recv()
+    for q in range(4):
+        span = pl.ds(q * quarter, quarter)
+        done = acc[:, span] + jnp.dot(
+            att[1, :, early:], w_rem[q, early:, :], preferred_element_type=jnp.float32
+        )
+        out_ref[:, span] = (done * gate_ref[:, span]).astype(out_ref.dtype)
+
+    @pl.loop(0, chunks)
+    def _(c):
+        side(c).wait_send()
+        att_copy(c).wait_send()
+
+        @pl.when(has_high)
+        def _():
+            up(c).wait_send()
+            side_high(c).wait_send()
+
+        @pl.when(has_low)
+        def _():
+            down(c).wait_send()
+            side_low(c).wait_send()
+
+    @pl.loop(0, WEIGHT_PIECES)
+    def _(p):
+        w_across(p).wait_send()
+        w_other(p).wait_send()
+        w_side(p).wait_send()
+        w_side_other(p).wait_send()
+
+
+def fused(queries, keys, values, kv_list, kv_count, out_weight, gate):
+    rows, width = queries.shape
+    cols = HEADS_PER_CHUNK * HD
+    chunks = width // cols
+    dma = pltpu.SemaphoreType.DMA
+    anywhere = pl.BlockSpec(memory_space=pl.ANY)
+    scalar = pl.BlockSpec(memory_space=pltpu.SMEM)
+    vector = pl.BlockSpec(memory_space=pltpu.VMEM)
+    return pl.pallas_call(
+        fused_kernel,
+        out_shape=jax.ShapeDtypeStruct((rows, width), jnp.bfloat16),
+        in_specs=[anywhere, anywhere, anywhere, scalar, scalar, anywhere, vector],
+        out_specs=vector,
+        scratch_shapes=[
+            pltpu.VMEM((rows, width), jnp.bfloat16),
+            pltpu.VMEM((6, chunks, 2, rows, cols), jnp.bfloat16),
+            pltpu.VMEM((2, rows, width), jnp.bfloat16),
+            pltpu.VMEM((width, width), jnp.bfloat16),
+            pltpu.VMEM((4, width, width // 4), jnp.bfloat16),
+            pltpu.VMEM((rows, width), jnp.float32),
+            dma((chunks, 2)),
+            dma,
+            dma,
+            dma((5, chunks)),
+            dma((6, chunks)),
+            dma((chunks,)),
+            dma((chunks,)),
+            dma((4, WEIGHT_PIECES)),
+            dma((4, WEIGHT_PIECES)),
+        ],
+        compiler_params=pltpu.CompilerParams(
+            collective_id=0, has_side_effects=True, vmem_limit_bytes=56 * 1024 * 1024
+        ),
+    )(queries, keys, values, kv_list, kv_count, out_weight, gate.reshape(1, -1))
+
+
 def solution(mesh):
+    shape = mesh.shape
+    paired = shape["head"] == 2 and shape["groups"] == 2 and shape["sub"] == 2
+
+    def body(queries, keys, values, kv_list, kv_count, out_weight, gate):
+        chosen = fused if paired and kv_list.shape[0] == 1 else local
+        return chosen(queries, keys, values, kv_list, kv_count, out_weight, gate)
+
     return jax.shard_map(
-        local,
+        body,
         mesh=mesh,
         in_specs=(
             P(("groups", "seq", "sub"), "head"),

time: 283 us -> 73.5 us (0.26)
  waiting for transfers between devices: 153 us -> 0 us
  Pallas kernels: 0 us -> 68.7 us
  matrix products: 52.7 us -> 0 us
  other arithmetic: 21.3 us -> 0 us
  between operations: 18.6 us -> 0.66 us
  starting transfers between devices: 17.1 us -> 0 us
  local copies, waits for them, and re-layouts: 19.6 us -> 3.65 us
    ppermute x6 -> x0, waiting for transfers between devices: 77.7 us -> none  [shifted(): return lax.ppermute(block, axis, route)]
    reduce_scatter x1 -> x0, waiting for transfers between devices: 75.6 us -> none  [local(): lax.psum_scatter(lax.dot_general(out_weight, attention, (((0,), (1,)), ((...]
    pallas_call x0 -> x1, Pallas kernels: none -> 68.7 us  [fused(): pl.pallas_call(fused_kernel, out_shape=jax.ShapeDtypeStruct((rows, width)...]
    dot_general x15 -> x0, matrix products: 52.7 us -> none  [the longest x7 26.8 us: local(): jnp.einsum('abhqk,bkhd->aqhd', weights.astype(jnp.bfloat16), value_tiles,...]
    ppermute x6 -> x0, starting transfers between devices: 17.1 us -> none  [shifted(): return lax.ppermute(block, axis, route)]
    reduce_sum x1 -> x0, other arithmetic: 16.3 us -> none  [local(): compute_total = compute_total + jnp.sum(weights, axis=(1, 4))]
    slice x6 -> x0, local copies, waits for them, and re-layouts: 15.1 us -> none  [the longest x5 13.9 us: local(): value_tiles = fetched[1].reshape(tiles_here, tile_rows, heads_here, HD)]
  transfers between devices with their start and end apart: 7 -> 0, of which waited for: 4 -> 0; matrix products, arithmetic and copies ran while one was open for 10% -> 0% of each run, Pallas kernels for 0% -> 0%
where the time goes in v1:
time: 73.5 us; the launch traced here: 73 us
  Pallas kernels  68.7 us (93%)
  local copies, waits for them, and re-layouts  3.65 us (5%)
    pallas_call x1, Pallas kernels, fused(): pl.pallas_call(fused_kernel, out_shape=jax.ShapeDtypeStruct((rows, width)...  68.7 us
    unnamed x1, local copies, waits for them, and re-layouts  2.36 us

profile of v1, /device:TPU:0, one launch (start us, length us, event | category | flops | bytes accessed | tf_op | source)
XLA Modules:
  0.0 73.0 jit_solution(1818397751361224876)
XLA Ops:
  0.7 1.3 %reshape.3.gate_ref = f32[1,1536]{1,0:T(1,128)} reshape(f32[1536]{0:T(1024)} %param.13) | data formatting | bytes 12288 | tf_op jit(solution)/shard_map/reshape | solution.py:424
  1.9 68.7 %shard_map.73 = bf16[384,1536]{1,0:T(8,128)(2,1)} custom-call(bf16[384,1536]{1,0:T(8,128)(2,1)} %q_hbm.1, bf16[384,1536]{1,0:T(8,128)(2,1)} %k_hbm.1, bf16[384,1536]{1,0:T(8,128)(2,1)} %v_hbm.1, s32[1,6]{1,0:T(1,128)} %list_ref.1, s32[1]{0:T(128)S(6)} %copy.9.count_ref, bf16[1536,3072]{1,0:T(8,128)(2,1)} %w_hbm.1, f32[1,1536]{1,0:T(1,128)} %reshape.3.gate_ref), custom_call_target="tpu_custom_call" | custom-call | tf_op jit(solution)/shard_map/pallas_call | solution.py:399
  70.6 2.4 %copy.10 = bf16[384,1536]{1,0:T(8,128)(2,1)} copy(bf16[384,1536]{1,0:T(8,128)(2,1)} %shard_map.73) | data formatting | bytes 2359296

commit v2 on v1

--- a/solution.py
+++ b/solution.py
@@ -94,9 +94,9 @@
     return (jnp.transpose(summed) * gate[None, :]).astype(jnp.bfloat16)
 
 
-HEADS_PER_CHUNK = 2
+HEADS_PER_CHUNK = 1
 AHEAD = 3
-WEIGHT_PIECES = 3
+WEIGHT_PIECES = 6
 MESH = pl.DeviceIdType.MESH
 
 
@@ -288,16 +288,16 @@
         def _():
             send_along(c + AHEAD)
 
-        @pl.when((c >= 1) & (c < 1 + WEIGHT_PIECES))
-        def _():
-            w_across(c - 1).wait_recv()
-            w_other(c - 1).start()
-            w_side(c - 1).start()
-
         @pl.when((c >= 3) & (c < 3 + WEIGHT_PIECES))
         def _():
-            w_other(c - 3).wait_recv()
-            w_side_other(c - 3).start()
+            w_across(c - 3).wait_recv()
+            w_other(c - 3).start()
+            w_side(c - 3).start()
+
+        @pl.when((c >= 6) & (c < 6 + WEIGHT_PIECES))
+        def _():
+            w_other(c - 6).wait_recv()
+            w_side_other(c - 6).start()
 
         arrived(1, c)
 
@@ -363,7 +363,7 @@
         done = acc[:, span] + jnp.dot(
             att[1, :, early:], w_rem[q, early:, :], preferred_element_type=jnp.float32
         )
-        out_ref[:, span] = (done * gate_ref[:, span]).astype(out_ref.dtype)
+        out_ref[:, span] = (done * gate_ref[span][None, :]).astype(out_ref.dtype)
 
     @pl.loop(0, chunks)
     def _(c):
@@ -421,7 +421,7 @@
         compiler_params=pltpu.CompilerParams(
             collective_id=0, has_side_effects=True, vmem_limit_bytes=56 * 1024 * 1024
         ),
-    )(queries, keys, values, kv_list, kv_count, out_weight, gate.reshape(1, -1))
+    )(queries, keys, values, kv_list, kv_count, out_weight, gate)
 
 
 def solution(mesh):

time: 73.5 us -> 71.6 us (0.974)
  local copies, waits for them, and re-layouts: 3.65 us -> 2.36 us
    reshape x1 -> x0, local copies, waits for them, and re-layouts: 1.29 us -> none  [fused(): gate.reshape(1, -1)]
where the time goes in v2:
time: 71.6 us; the launch traced here: 71.3 us
  Pallas kernels  68.3 us (95%)
  local copies, waits for them, and re-layouts  2.36 us (3%)
    pallas_call x1, Pallas kernels, fused(): pl.pallas_call(fused_kernel, out_shape=jax.ShapeDtypeStruct((rows, width)...  68.3 us
    unnamed x1, local copies, waits for them, and re-layouts  2.36 us

profile of v2, /device:TPU:0, one launch (start us, length us, event | category | flops | bytes accessed | tf_op | source)
XLA Modules:
  0.0 71.3 jit_solution(1345279998096852456)
XLA Ops:
  0.7 68.3 %shard_map.73 = bf16[384,1536]{1,0:T(8,128)(2,1)} custom-call(bf16[384,1536]{1,0:T(8,128)(2,1)} %q_hbm.1, bf16[384,1536]{1,0:T(8,128)(2,1)} %k_hbm.1, bf16[384,1536]{1,0:T(8,128)(2,1)} %v_hbm.1, s32[1,6]{1,0:T(1,128)} %list_ref.1, s32[1]{0:T(128)S(6)} %copy.9.count_ref, bf16[1536,3072]{1,0:T(8,128)(2,1)} %w_hbm.1, f32[1536]{0:T(1024)} %gate_ref.1), custom_call_target="tpu_custom_call" | custom-call | tf_op jit(solution)/shard_map/pallas_call | solution.py:399
  69.0 2.4 %copy.10 = bf16[384,1536]{1,0:T(8,128)(2,1)} copy(bf16[384,1536]{1,0:T(8,128)(2,1)} %shard_map.73) | data formatting | bytes 2359296

commit v3 on v2

--- a/solution.py
+++ b/solution.py
@@ -271,6 +271,7 @@
         biases.append(bias)
     factor = (1.0 / math.sqrt(HD)) * math.log2(math.e)
     q_copy.wait()
+    half = chunks // 2 * cols
 
     @pl.loop(0, chunks)
     def _(c):
@@ -298,6 +299,15 @@
         def _():
             w_other(c - 6).wait_recv()
             w_side_other(c - 6).start()
+
+        @pl.when(c == chunks // 2)
+        def _():
+            w_copy.wait()
+            for q in range(4):
+                span = pl.ds(q * quarter, quarter)
+                acc[:, span] = jnp.dot(
+                    att[0, :, :half], w_own[:half, span], preferred_element_type=jnp.float32
+                )
 
         arrived(1, c)
 
@@ -337,10 +347,11 @@
             att[0, :, place] = (mixed / total).astype(jnp.bfloat16)
         att_copy(c).start()
 
-    w_copy.wait()
     for q in range(4):
         span = pl.ds(q * quarter, quarter)
-        acc[:, span] = jnp.dot(att[0], w_own[:, span], preferred_element_type=jnp.float32)
+        acc[:, span] += jnp.dot(
+            att[0, :, half:], w_own[half:, span], preferred_element_type=jnp.float32
+        )
 
     @pl.loop(0, WEIGHT_PIECES)
     def _(p):

time: 71.6 us -> 71 us (level)
  no operation moved by 1% of the time
where the time goes in v3:
time: 71 us; the launch traced here: 70.8 us
  Pallas kernels  67.8 us (95%)
  local copies, waits for them, and re-layouts  2.36 us (3%)
    pallas_call x1, Pallas kernels, fused(): pl.pallas_call(fused_kernel, out_shape=jax.ShapeDtypeStruct((rows, width)...  67.8 us
    unnamed x1, local copies, waits for them, and re-layouts  2.36 us

profile of v3, /device:TPU:0, one launch (start us, length us, event | category | flops | bytes accessed | tf_op | source)
XLA Modules:
  0.0 70.8 jit_solution(10325252714536108665)
XLA Ops:
  0.7 67.8 %shard_map.73 = bf16[384,1536]{1,0:T(8,128)(2,1)} custom-call(bf16[384,1536]{1,0:T(8,128)(2,1)} %q_hbm.1, bf16[384,1536]{1,0:T(8,128)(2,1)} %k_hbm.1, bf16[384,1536]{1,0:T(8,128)(2,1)} %v_hbm.1, s32[1,6]{1,0:T(1,128)} %list_ref.1, s32[1]{0:T(128)S(6)} %copy.9.count_ref, bf16[1536,3072]{1,0:T(8,128)(2,1)} %w_hbm.1, f32[1536]{0:T(1024)} %gate_ref.1), custom_call_target="tpu_custom_call" | custom-call | tf_op jit(solution)/shard_map/pallas_call | solution.py:410
  68.4 2.4 %copy.10 = bf16[384,1536]{1,0:T(8,128)(2,1)} copy(bf16[384,1536]{1,0:T(8,128)(2,1)} %shard_map.73) | data formatting | bytes 2359296
